TPU v7x, 32 devices: a whole 2x2x4 slice. The times are simulated.
32 devices in a mesh: row: 4 (over z), col: 8 (over y, x, core).
Axes of the slice: x: 2, y: 2, z: 4, core: 2. Of those that a mesh axis runs over, the one named last changes fastest.
Arguments:
- slot_factors: bfloat16 [4, 8, 2, 1024, 256], P('row', 'col'), may hold values from -0.75 to 0.75
- slot_pairs: int32 [4, 8, 2], P('row', 'col'), may hold values from 0 to 2, as said below
- pivot_factors: bfloat16 [8, 1024, 256], P('row', 'col'), may hold values from -0.75 to 0.75
- a_factors: bfloat16 [8, 1024, 256], P('col'), as said below
- diag_factor: float32 [1024, 1024], replicated, as said below
- sketch: float32 [1024, 128], replicated, as said below
Outputs:
- panel_basis: float32 [8, 1024, 128], P('col')
- panel_coeff: float32 [8, 1024, 128], P('col')
Inputs may be any that keep to these rules, and one draw needn't show every extreme that they name: `slot_pairs`: on each cell (r, c) the live codes come first, are distinct and below 2; the remaining entries equal 2. Every cell has at least one live slot, and in every draw some cell is full and some cell has exactly one. `diag_factor`: lower triangular; the diagonal lies between 1 and 2. `a_factors`: real values of order one. `sketch`: real values.
All inputs are finite; a program needn't handle non-finite values.
Results may differ from a plain program's by a relative error of at most 0.0003.
Values may be sent and summed in bfloat16 or wider, within the bound.
A program may use at most 64 MiB of HBM per device.

v0:
```python
import jax
import jax.numpy as jnp
from jax import lax
from jax.sharding import PartitionSpec as P


def orthonormal_rows(sketch_rows, gram_matrix):
    factor_low = jnp.linalg.cholesky(gram_matrix)
    solved = lax.linalg.triangular_solve(
        factor_low, jnp.swapaxes(sketch_rows, 1, 2), left_side=True, lower=True
    )
    return jnp.swapaxes(solved, 1, 2)


def shards(slot_factors, slot_pairs, pivot_factors, a_factors, diag_factor, sketch):
    precise_mode = lax.Precision.HIGHEST
    tile_size = sketch.shape[0]
    rank_size = sketch.shape[1]
    tile_rows = a_factors.shape[0]
    earlier = pivot_factors.shape[0]
    pivot_data = lax.all_gather(pivot_factors, "col", axis=1, tiled=True).astype(jnp.float32)
    pivot_left_factor = pivot_data[..., :rank_size]
    pivot_right_factor = pivot_data[..., rank_size:]
    weights = jnp.einsum("jbr,bc->jrc", pivot_left_factor, sketch, precision=precise_mode)
    slot_data = slot_factors[0, 0].astype(jnp.float32)
    slot_left_factor = slot_data[..., :rank_size]
    slot_right_factor = slot_data[..., rank_size:]
    pair_codes = slot_pairs[0, 0]
    tile_selector = jax.nn.one_hot(pair_codes // earlier, tile_rows, dtype=jnp.float32)
    column_selector = jax.nn.one_hot(pair_codes % earlier, earlier, dtype=jnp.float32)
    slot_pivot_right_factor = jnp.einsum(
        "kf,fed->ked", column_selector, pivot_right_factor, precision=precise_mode
    )
    coupling_matrix = jnp.einsum(
        "jzk,jzu->jku", slot_right_factor, slot_pivot_right_factor, precision=precise_mode
    )
    slot_weights = jnp.einsum("sj,jrc->src", column_selector, weights, precision=precise_mode)
    panel_kernel = jnp.einsum("src,scd->srd", coupling_matrix, slot_weights, precision=precise_mode)
    update_contribution = jnp.einsum(
        "gxn,gny->gxy", slot_left_factor, panel_kernel, precision=precise_mode
    )
    y_part = jnp.einsum("st,sbd->tbd", tile_selector, update_contribution, precision=precise_mode)
    a_data = a_factors.astype(jnp.float32)
    a_left = a_data[..., :rank_size]
    a_right = a_data[..., rank_size:]
    a_sketch = jnp.einsum("ibr,bc->irc", a_right, sketch, precision=precise_mode)
    y_a = jnp.einsum("ibr,irc->ibc", a_left, a_sketch, precision=precise_mode)
    sketch_rows = y_a - lax.psum(y_part, "row")
    gram_matrix = jnp.einsum("ibr,ibc->irc", sketch_rows, sketch_rows, precision=precise_mode)
    basis_column_count = orthonormal_rows(sketch_rows, gram_matrix)
    slot_basis_matrix = jnp.einsum(
        "hw,wlf->hlf", tile_selector, basis_column_count, precision=precise_mode
    )
    slot_pivot_left_factor = jnp.einsum(
        "kf,fed->ked", column_selector, pivot_left_factor, precision=precise_mode
    )
    inner_product = jnp.einsum(
        "jzk,jzu->jku", slot_left_factor, slot_basis_matrix, precision=precise_mode
    )
    reduced = jnp.einsum("src,srd->scd", coupling_matrix, inner_product, precision=precise_mode)
    lifted = jnp.einsum("sbc,scd->sbd", slot_pivot_left_factor, reduced, precision=precise_mode)
    m_part = jnp.einsum("st,sbd->tbd", tile_selector, lifted, precision=precise_mode)
    m_sum = lax.psum(m_part, "row")
    a_inner = jnp.einsum("ibr,ibc->irc", a_left, basis_column_count, precision=precise_mode)
    m_a = jnp.einsum("ibr,irc->ibc", a_right, a_inner, precision=precise_mode)
    projected = m_a - m_sum
    stacked = jnp.transpose(projected, (1, 0, 2)).reshape(tile_size, tile_rows * rank_size)
    solved = lax.linalg.triangular_solve(diag_factor, stacked, left_side=True, lower=True)
    coefficient = jnp.transpose(solved.reshape(tile_size, tile_rows, rank_size), (1, 0, 2))
    root_tile = jnp.sqrt(jnp.float32(tile_size))
    return (basis_column_count * root_tile, coefficient / root_tile)


def solution(mesh):
    in_specs = (
        P("row", "col", None, None, None),
        P("row", "col", None),
        P("row", "col", None),
        P("col", None, None),
        P(),
        P(),
    )
    out_specs = (P("col", None, None), P("col", None, None))
    return jax.shard_map(shards, mesh=mesh, in_specs=in_specs, out_specs=out_specs, check_vma=False)
```

profile of v0, /device:TPU:28, one launch (start us, length us, event | category | flops | bytes accessed | tf_op | source)
XLA Modules:
  0.0 243.0 jit_solution(9842760754554709494)
XLA Ops:
  7.2 0.7 all-gather.2.cloned.1.call-update
  8.0 0.7 and_select_fusion.1
  8.6 0.7 compare_convert_fusion.1
  9.3 0.7 fusion.77
  10.0 4.7 %fusion = f32[1024,1024]{1,0:T(8,128)} fusion(f32[1024,1024]{1,0:T(8,128)} %param.10), kind=kLoop, calls=%fused_computation.3 | loop fusion | flops 2097152 | bytes 8388608 | tf_op jit(solution)/shard_map/triangular_solve | solution.py:68
  14.7 19.7 %all-gather.2.cloned.1.call-done = bf16[2,1024,256]{2,1,0:T(8,128)(2,1)} async-done(((bf16[2,128,256]{2,1,0:T(8,128)(2,1)}), bf16[2,1024,256]{2,1,0:T(8,128)(2,1)}) %all-gather.2.cloned.1.call-update) | async-done | bytes 1048592 | tf_op jit(solution)/shard_map/all_gather | solution.py:21
  34.3 1.7 fusion.19
  36.5 1.3 fusion.85
  37.8 0.8 fusion.25
  38.6 1.0 fusion.8
  40.0 1.4 fusion.2
  42.2 1.7 fusion.23
  43.9 35.1 %all-reduce.3.cloned.1.call-done = f32[1,1024,128]{1,2,0:T(8,128)} async-done(((f32[1,1024,128]{1,2,0:T(8,128)}), f32[1,1024,128]{1,2,0:T(8,128)}) %all-reduce.3.cloned.1.call-update) | async-done | bytes 524304 | tf_op jit(solution)/shard_map/psum | solution.py:48
  79.0 1.5 fusion.3
  80.5 0.6 fusion.17
  81.2 11.7 %custom-call.10 = f32[1,128,128]{2,1,0:T(8,128)S(1)} custom-call(f32[1,128,128]{2,1,0:T(8,128)S(1)} %fusion.73), custom_call_target="Cholesky" | custom-call | tf_op jit(solution)/shard_map/jit(cholesky)/cholesky | solution.py:8
  92.9 0.6 compare_reduce_fusion
  93.6 0.7 fusion.64
  94.2 9.8 %custom-call.11 = f32[1,1,128,128]{2,3,1,0:T(8,128)S(1)} custom-call(f32[1,1,128,128]{3,2,1,0:T(8,128)S(1)} %fusion.64), custom_call_target="InvertDiagBlocksLowerTriangular" | custom-call | tf_op jit(solution)/shard_map/triangular_solve | solution.py:9
  104.0 0.6 bitcast_multiply_fusion
  104.9 1.1 fusion.10
  106.4 2.2 fusion.6
  108.6 2.7 %fusion.12 = f32[1,1024,128]{2,0,1:T(1,128)S(1)} fusion(f32[2,1024,128]{2,1,0:T(8,128)S(1)} %fusion.6, s32[1,1,2]{2,1,0:T(1,128)S(1)} %copy-done.4), kind=kOutput, calls=%fused_computation.26 | convolution fusion | flops 3145760 | bytes 1572872 | tf_op jit(solution)/shard_map/st,sbd->tbd/dot_general | solution.py:62
  111.4 1.0 copy.23
  112.4 27.7 %while.1 = (s32[]{:T(128)}, f32[1024,1024]{1,0:T(8,128)}, s32[8,2]{0,1:T(2,128)S(1)}, f32[8,128,128]{2,1,0:T(8,128)}, s32[]{:T(128)}) while((s32[]{:T(128)}, f32[1024,1024]{1,0:T(8,128)}, s32[8,2]{0,1:T(2,128)S(1)}, f32[8,128,128]{2,1,0:T(8,128)}, s32[]{:T(128)}) %tuple.44), condition=%wide.while_cond, body=%wide.while_body.sunk | while | flops 2 | bytes 132205 | solution.py:68
  112.5 0.6 fusion.108
  113.1 2.8 %bitcast_dynamic-update-slice_fusion.9 = f32[8,128,128]{2,1,0:T(8,128)} fusion(f32[8,128,128]{2,1,0:T(8,128)} %get-tuple-element.94, s32[]{:T(128)S(6)} %copy.43, f32[1024,1024]{1,0:T(8,128)} %get-tuple-element.97, s32[]{:T(128)} %bitcast.210, s32[]{:T(128)} %bitcast.211), kind=kLoop, calls=%fused_computation.clone.1 | loop fusion | bytes 132100 | tf_op jit(solution)/shard_map/triangular_solve
  116.0 0.6 fusion.108
  116.6 2.8 %bitcast_dynamic-update-slice_fusion.9 = f32[8,128,128]{2,1,0:T(8,128)} fusion(f32[8,128,128]{2,1,0:T(8,128)} %get-tuple-element.94, s32[]{:T(128)S(6)} %copy.43, f32[1024,1024]{1,0:T(8,128)} %get-tuple-element.97, s32[]{:T(128)} %bitcast.210, s32[]{:T(128)} %bitcast.211), kind=kLoop, calls=%fused_computation.clone.1 | loop fusion | bytes 132100 | tf_op jit(solution)/shard_map/triangular_solve
  119.4 0.6 fusion.108
  120.0 2.8 %bitcast_dynamic-update-slice_fusion.9 = f32[8,128,128]{2,1,0:T(8,128)} fusion(f32[8,128,128]{2,1,0:T(8,128)} %get-tuple-element.94, s32[]{:T(128)S(6)} %copy.43, f32[1024,1024]{1,0:T(8,128)} %get-tuple-element.97, s32[]{:T(128)} %bitcast.210, s32[]{:T(128)} %bitcast.211), kind=kLoop, calls=%fused_computation.clone.1 | loop fusion | bytes 132100 | tf_op jit(solution)/shard_map/triangular_solve
  122.9 0.6 fusion.108
  123.5 2.8 %bitcast_dynamic-update-slice_fusion.9 = f32[8,128,128]{2,1,0:T(8,128)} fusion(f32[8,128,128]{2,1,0:T(8,128)} %get-tuple-element.94, s32[]{:T(128)S(6)} %copy.43, f32[1024,1024]{1,0:T(8,128)} %get-tuple-element.97, s32[]{:T(128)} %bitcast.210, s32[]{:T(128)} %bitcast.211), kind=kLoop, calls=%fused_computation.clone.1 | loop fusion | bytes 132100 | tf_op jit(solution)/shard_map/triangular_solve
  127.0 2.8 %bitcast_dynamic-update-slice_fusion.9 = f32[8,128,128]{2,1,0:T(8,128)} fusion(f32[8,128,128]{2,1,0:T(8,128)} %get-tuple-element.94, s32[]{:T(128)S(6)} %copy.43, f32[1024,1024]{1,0:T(8,128)} %get-tuple-element.97, s32[]{:T(128)} %bitcast.210, s32[]{:T(128)} %bitcast.211), kind=kLoop, calls=%fused_computation.clone.1 | loop fusion | bytes 132100 | tf_op jit(solution)/shard_map/triangular_solve
  130.4 2.8 %bitcast_dynamic-update-slice_fusion.9 = f32[8,128,128]{2,1,0:T(8,128)} fusion(f32[8,128,128]{2,1,0:T(8,128)} %get-tuple-element.94, s32[]{:T(128)S(6)} %copy.43, f32[1024,1024]{1,0:T(8,128)} %get-tuple-element.97, s32[]{:T(128)} %bitcast.210, s32[]{:T(128)} %bitcast.211), kind=kLoop, calls=%fused_computation.clone.1 | loop fusion | bytes 132100 | tf_op jit(solution)/shard_map/triangular_solve
  133.9 2.8 %bitcast_dynamic-update-slice_fusion.9 = f32[8,128,128]{2,1,0:T(8,128)} fusion(f32[8,128,128]{2,1,0:T(8,128)} %get-tuple-element.94, s32[]{:T(128)S(6)} %copy.43, f32[1024,1024]{1,0:T(8,128)} %get-tuple-element.97, s32[]{:T(128)} %bitcast.210, s32[]{:T(128)} %bitcast.211), kind=kLoop, calls=%fused_computation.clone.1 | loop fusion | bytes 132100 | tf_op jit(solution)/shard_map/triangular_solve
  137.3 2.7 %bitcast_dynamic-update-slice_fusion.9 = f32[8,128,128]{2,1,0:T(8,128)} fusion(f32[8,128,128]{2,1,0:T(8,128)} %get-tuple-element.94, s32[]{:T(128)S(6)} %copy.43, f32[1024,1024]{1,0:T(8,128)} %get-tuple-element.97, s32[]{:T(128)} %bitcast.210, s32[]{:T(128)} %bitcast.211), kind=kLoop, calls=%fused_computation.clone.1 | loop fusion | bytes 132100 | tf_op jit(solution)/shard_map/triangular_solve
  140.1 79.4 %custom-call.12 = f32[8,128,128]{1,2,0:T(8,128)S(1)} custom-call(f32[8,128,128]{2,1,0:T(8,128)} %get-tuple-element.9), custom_call_target="InvertDiagBlocksLowerTriangular" | custom-call | tf_op jit(solution)/shard_map/triangular_solve | solution.py:68
  219.5 1.0 copy.11
  220.9 1.4 fusion.4
  222.6 1.1 convolution_subtract_fusion.4
  224.1 1.3 convolution_subtract_fusion.3
  225.7 1.4 convolution_subtract_fusion.6
  227.4 1.5 convolution_subtract_fusion.5
  229.3 1.7 convolution_subtract_fusion.2
  231.3 1.8 convolution_subtract_fusion.1
  233.4 1.9 convolution_subtract_fusion
  235.7 0.8 broadcast_multiply_fusion
  (55 shorter events, 8.0 us)
Async XLA Ops:
  7.2 27.2 %copy-start = (f32[1024,128]{1,0:T(8,128)S(1)}, f32[1024,128]{1,0:T(8,128)}, u32[]{:S(2)}) copy-start(f32[1024,128]{1,0:T(8,128)} %param.11) | copy-start | bytes 1572868
  7.2 27.2 %all-gather.2.cloned.1.call-start = ((), (), s32[]{:S(2)}) async-start(), calls=%async_computation | async-start | bytes 1179648 | tf_op jit(solution)/shard_map/all_gather | solution.py:21
  7.9 71.1 %all-reduce.3.cloned.1.call-start = ((), (), s32[]{:S(2)}) async-start(), calls=%async_computation.1 | async-start | bytes 1048576 | tf_op jit(solution)/shard_map/psum | solution.py:48
  14.7 23.9 %copy-start.1 = (bf16[1,1,2,1024,256]{4,3,2,1,0:T(8,128)(2,1)S(1)}, bf16[1,1,2,1024,256]{4,3,2,1,0:T(8,128)(2,1)}, u32[]{:S(2)}) copy-start(bf16[1,1,2,1024,256]{4,3,2,1,0:T(8,128)(2,1)} %param.6) | copy-start | bytes 3145732
  36.1 5.6 %copy-start.2 = (bf16[1,1024,256]{2,1,0:T(8,128)(2,1)S(1)}, bf16[1,1024,256]{2,1,0:T(8,128)(2,1)}, u32[]{:S(2)}) copy-start(bf16[1,1024,256]{2,1,0:T(8,128)(2,1)} %param.9) | copy-start | bytes 1572868
  41.5 179.5 %all-reduce.5.cloned.1.call-start = ((), (), s32[]{:S(2)}) async-start(), calls=%async_computation.2 | async-start | bytes 1048576 | tf_op jit(solution)/shard_map/psum | solution.py:63
  43.9 64.7 %copy-start.4 = (s32[1,1,2]{2,1,0:T(1,128)S(1)}, s32[1,1,2]{2,1,0:T(1,128)}, u32[]{:S(2)}) copy-start(s32[1,1,2]{2,1,0:T(1,128)} %param.7) | copy-start | bytes 28
  106.0 114.5 %copy-start.3 = (bf16[1,1024,256]{2,1,0:T(8,128)(2,1)S(1)}, bf16[1,1024,256]{2,1,0:T(8,128)(2,1)}, u32[]{:S(2)}) copy-start(bf16[1,1024,256]{2,1,0:T(8,128)(2,1)} %param.9) | copy-start | bytes 1572868
Sparse Core Ops, SparseCore 0:
  9.9 24.3 all-gather.1
  41.6 37.3 all-reduce.2
  112.5 38.3 all-reduce.4
where the time goes:
time: 247 us; the launch traced here: 243 us
  other arithmetic  110 us (45%)
  waiting for transfers between devices  55.5 us (22%)
  matrix products  31.9 us (13%)
  local copies, waits for them, and re-layouts  31.4 us (13%)
  between operations  14.1 us (6%)
    another operation x3, other arithmetic, shards(): lax.linalg.triangular_solve(diag_factor, stacked, left_side=True, lower=T...  84.1 us
    psum x1, waiting for transfers between devices, shards(): sketch_rows = y_a - lax.psum(y_part, 'row')  35.1 us
    another operation x25, local copies, waits for them, and re-layouts  27.8 us
    all_gather x1, waiting for transfers between devices, shards(): lax.all_gather(pivot_factors, 'col', axis=1, tiled=True).astype(jnp.float32)  19.7 us
    another operation x15, matrix products, shards(): lax.linalg.triangular_solve(diag_factor, stacked, left_side=True, lower=T...  13.1 us
    another operation x3, other arithmetic, orthonormal_rows(): factor_low = jnp.linalg.cholesky(gram_matrix)  12.4 us
    another operation x2, other arithmetic, orthonormal_rows(): lax.linalg.triangular_solve(factor_low, jnp.swapaxes(sketch_rows, 1, 2),...  10.5 us
  transfers between devices with their start and end apart: 3, of which 2 were waited for; matrix products, arithmetic and copies ran while one was open for 48% of the time, Pallas kernels for 0%

commit v1 on v0

v1 whole, which is shorter than its diff:
```python
import functools

import jax
import jax.numpy as jnp
from jax import lax
from jax.experimental import pallas as pl
from jax.experimental.pallas import tpu as pltpu
from jax.sharding import PartitionSpec as P

MESH = pl.DeviceIdType.MESH
F32 = jnp.float32
BF16 = jnp.bfloat16
NN = (((1,), (0,)), ((), ()))
TN = (((0,), (0,)), ((), ()))
NT = (((1,), (1,)), ((), ()))


def split(x):
    high = x.astype(BF16)
    return high, (x - high.astype(F32)).astype(BF16)


def dot(a, b, dims=NN):
    return lax.dot_general(a, b, dims, preferred_element_type=F32)


def dot_exact_left(a, b, dims=NN):
    high, low = split(b)
    return dot(a, high, dims) + dot(a, low, dims)


def dot_split(a, b, dims=NN):
    a_high, a_low = a
    b_high, b_low = b
    return dot(a_high, b_high, dims) + (dot(a_high, b_low, dims) + dot(a_low, b_high, dims))


def dot_wide(a, b, dims=NN):
    return dot_split(split(a), split(b), dims)


def kernel(
    n_row, n_col,
    slot_ref, pairs_ref, pivot_ref, a_ref, diag_ref, sketch_ref,
    basis_ref, coeff_ref,
    diag_v, inv_small, inv_high, inv_low, pv_all, pu_all, coupling,
    y_own, y_part, y_in, y_full, x_all, hinv,
    diag_sem, pv_send, pv_recv, pu_send, pu_recv, pz_send, pz_recv,
    pf_send, pf_recv, rs_send, rs_recv, ag_send, ag_recv, x_send, x_recv,
):
    tile, rank = sketch_ref.shape
    columns, rows = pivot_ref.shape[0], pivot_ref.shape[1]
    slots = slot_ref.shape[2]
    chunk = tile // n_row
    r = lax.axis_index("row")
    c = lax.axis_index("col")

    diag_copy = pltpu.make_async_copy(diag_ref, diag_v, diag_sem)
    diag_copy.start()

    def piece(index):
        return pl.ds(pl.multiple_of(index * rows, rows), rows)

    def part(index):
        return pl.ds(pl.multiple_of(index * chunk, chunk), chunk)

    for j in range(columns):
        lanes = slice(j * rank, (j + 1) * rank)
        pu_all[r, piece(c), lanes] = pivot_ref[j, :, :rank]
        pv_all[piece(c), lanes] = pivot_ref[j, :, rank:]

    barrier = pltpu.get_barrier_semaphore()

    def greet_col(d, _):
        pl.semaphore_signal(barrier, inc=1, device_id={"col": lax.rem(c + d, n_col)}, device_id_type=MESH)
        return 0

    def greet_row(d, _):
        pl.semaphore_signal(barrier, inc=1, device_id={"row": lax.rem(r + d, n_row)}, device_id_type=MESH)
        return 0

    lax.fori_loop(1, n_col, greet_col, 0)
    lax.fori_loop(1, n_row, greet_row, 0)
    pl.semaphore_wait(barrier, n_col - 1 + n_row - 1)

    def to_col(ref, send, recv, d):
        return pltpu.make_async_remote_copy(
            ref, ref, send, recv, device_id={"col": lax.rem(c + d, n_col)}, device_id_type=MESH
        )

    def to_row(source, target, send, recv, d):
        return pltpu.make_async_remote_copy(
            source, target, send, recv, device_id={"row": lax.rem(r + d, n_row)}, device_id_type=MESH
        )

    def pv_copy(d, index):
        return to_col(pv_all.at[piece(index)], pv_send.at[d - 1], pv_recv.at[d - 1], d)

    def pu_copy(d, index):
        return to_col(pu_all.at[r, piece(index)], pu_send.at[d - 1], pu_recv.at[d - 1], d)

    def pz_copy(d, index):
        ref = pu_all.at[index, piece(c)]
        return to_row(ref, ref, pz_send.at[d - 1], pz_recv.at[d - 1], d)

    def pf_copy(e, d, index):
        from_row = lax.rem(r + n_row - e, n_row)
        return to_col(
            pu_all.at[from_row, piece(index)], pf_send.at[e - 1, d - 1], pf_recv.at[e - 1, d - 1], d
        )

    def rs_copy(d):
        return to_row(
            y_part.at[part(lax.rem(r + d, n_row))], y_in.at[d - 1], rs_send.at[d - 1], rs_recv.at[d - 1], d
        )

    def ag_copy(d, index):
        ref = y_full.at[part(index)]
        return to_row(ref, ref, ag_send.at[d - 1], ag_recv.at[d - 1], d)

    def x_copy(d, index):
        ref = x_all.at[index]
        return to_row(ref, ref, x_send.at[d - 1], x_recv.at[d - 1], d)

    def col_source(d):
        return lax.rem(c + n_col - d, n_col)

    def row_source(d):
        return lax.rem(r + n_row - d, n_row)

    def each(n, act):
        def body(d, _):
            act(d)
            return 0

        lax.fori_loop(1, n, body, 0)

    def push_pivots(d):
        pv_copy(d, c).start()
        pu_copy(d, c).start()

    each(n_col, push_pivots)
    each(n_row, lambda d: pz_copy(d, r).start())

    sketch_split = split(sketch_ref[...])
    a_left = a_ref[0, :, :rank]
    a_right = a_ref[0, :, rank:]
    a_sketch = dot(a_right, sketch_split[0], TN) + dot(a_right, sketch_split[1], TN)
    y_own[...] = dot_exact_left(a_left, a_sketch)

    diag_copy.wait()
    blocks = tile // rank
    sub = lax.broadcasted_iota(jnp.int32, (rank, rank), 0)
    lane = lax.broadcasted_iota(jnp.int32, (rank, rank), 1)
    on_diag = sub == lane

    def diag_block(b):
        span = slice(b * rank, (b + 1) * rank)
        return diag_v[span, span]

    for b in range(blocks):
        low = diag_block(b)
        only = jnp.where(on_diag, low, 0.0)
        inv_sub = 1.0 / jnp.sum(only, axis=1, keepdims=True)
        inv_lane = 1.0 / jnp.sum(only, axis=0, keepdims=True)
        pair = (sub == lane + 1) & ((lane & 1) == 0)
        inv_small[b] = jnp.where(on_diag, inv_lane, 0.0) - jnp.where(pair, low * inv_sub * inv_lane, 0.0)

    def double(level, _):
        step = (lax.shift_right_logical(sub, level + 1) == lax.shift_right_logical(lane, level + 1)) & (
            lax.shift_right_logical(sub, level) != lax.shift_right_logical(lane, level)
        )
        for b in range(blocks):
            now = inv_small[b]
            now_split = split(now)
            cross = split(jnp.where(step, diag_block(b), 0.0))
            inv_small[b] = now - dot_split(split(dot_split(now_split, cross)), now_split)
        return 0

    lax.fori_loop(1, rank.bit_length() - 1, double, 0)

    each(n_col, lambda d: pv_copy(d, col_source(d)).wait_recv())
    each(n_col, lambda d: pu_copy(d, col_source(d)).wait_recv())
    pivot_right = pv_all[...]
    for s in range(slots):
        code = pairs_ref[0, 0, s]
        coupled = dot(slot_ref[0, 0, s, :, rank:], pivot_right, TN)
        for j in range(columns):
            lanes = slice(j * rank, (j + 1) * rank)
            coupling[s * rank:(s + 1) * rank, lanes] = jnp.where(code == j, coupled[:, lanes], 0.0)
    pivot_left = pu_all[r]
    weights = dot(pivot_left, sketch_split[0], TN) + dot(pivot_left, sketch_split[1], TN)
    mixed = dot_wide(coupling[...], weights)
    total = dot_exact_left(slot_ref[0, 0, 0, :, :rank], mixed[:rank])
    for s in range(1, slots):
        total += dot_exact_left(slot_ref[0, 0, s, :, :rank], mixed[s * rank:(s + 1) * rank])
    y_part[...] = total
    each(n_row, lambda d: rs_copy(d).start())

    def forward(e):
        pz_copy(e, row_source(e)).wait_recv()
        each(n_col, lambda d: pf_copy(e, d, c).start())

    each(n_row, forward)

    inv_high[...] = jnp.zeros_like(inv_high)
    inv_low[...] = jnp.zeros_like(inv_low)
    for b in range(blocks):
        span = slice(b * rank, (b + 1) * rank)
        high, low = split(inv_small[b])
        inv_high[span, span] = high
        inv_low[span, span] = low
    size = rank
    while size < tile:
        for start in range(0, tile, 2 * size):
            first = slice(start, start + size)
            second = slice(start + size, start + 2 * size)
            middle = dot_split(split(diag_v[second, first]), (inv_high[first, first], inv_low[first, first]))
            cross = dot_split((inv_high[second, second], inv_low[second, second]), split(middle))
            high, low = split(-cross)
            inv_high[second, first] = high
            inv_low[second, first] = low
        size *= 2

    each(n_row, lambda d: rs_copy(d).wait_recv())
    mine = y_own[part(r)] - y_part[part(r)]
    for d in range(1, n_row):
        mine = mine - y_in[d - 1]
    y_full[part(r)] = mine
    each(n_row, lambda d: ag_copy(d, r).start())
    each(n_row, lambda d: ag_copy(d, row_source(d)).wait_recv())

    sketched = y_full[...]
    sketched_split = split(sketched)
    gram = lax.dot_general(sketched, sketched, TN, precision=lax.Precision.HIGHEST, preferred_element_type=F32)
    state = jnp.concatenate([gram, jnp.where(on_diag, 1.0, 0.0)], axis=1)
    group = 8
    sub_group = lax.broadcasted_iota(jnp.int32, (group, 1), 0)
    lane_group = lax.broadcasted_iota(jnp.int32, (group, 2 * rank), 1)
    sub_wide = lax.broadcasted_iota(jnp.int32, (group, 2 * rank), 0)
    for start in range(0, rank, group):
        block = state[start:start + group]
        for t in range(group - 1):
            k = start + t
            factor = block[:, k:k + 1] / block[t:t + 1, k:k + 1]
            block = block - jnp.where(sub_group > t, factor, 0.0) * block[t:t + 1]
        pivots = jnp.sum(jnp.where(lane_group == sub_wide + start, block, 0.0), axis=1, keepdims=True)
        block = block * lax.rsqrt(pivots)
        hinv[start:start + group] = block[:, rank:]
        if start + group < rank:
            left = jnp.where(lane_group[:, :rank] >= start + group, block[:, :rank], 0.0)
            state = state - dot_wide(left, block, TN)

    basis_split = split(dot_split(sketched_split, split(hinv[...]), NT))
    basis = basis_split[0].astype(F32) + basis_split[1].astype(F32)

    def across(left):
        return dot(left, basis_split[0], TN) + dot(left, basis_split[1], TN)

    inner = jnp.concatenate([across(slot_ref[0, 0, s, :, :rank]) for s in range(slots)], axis=0)
    x_all[r] = dot_wide(coupling[...], inner, TN)
    each(n_row, lambda d: x_copy(d, r).start())

    root = float(tile) ** 0.5
    basis_ref[0] = basis * root
    projected = dot_exact_left(a_right, across(a_left))
    each(n_row, lambda e: each(n_col, lambda d: pf_copy(e, d, col_source(d)).wait_recv()))
    each(n_row, lambda d: x_copy(d, row_source(d)).wait_recv())
    for row in range(n_row):
        projected = projected - dot_exact_left(pu_all[row], x_all[row])
    projected_split = split(projected)
    coeff_ref[0] = dot_split((inv_high[...], inv_low[...]), projected_split) * (1.0 / root)

    def finish_col(d):
        pv_copy(d, c).wait_send()
        pu_copy(d, c).wait_send()

    def finish_row(d):
        pz_copy(d, r).wait_send()
        rs_copy(d).wait_send()
        ag_copy(d, r).wait_send()
        x_copy(d, r).wait_send()

    each(n_col, finish_col)
    each(n_row, finish_row)
    each(n_row, lambda e: each(n_col, lambda d: pf_copy(e, d, c).wait_send()))


def solution(mesh):
    n_row, n_col = mesh.shape["row"], mesh.shape["col"]

    def shards(slot_factors, slot_pairs, pivot_factors, a_factors, diag_factor, sketch):
        tile, rank = sketch.shape
        columns, rows = pivot_factors.shape[:2]
        slots = slot_factors.shape[2]
        chunk = tile // n_row
        vmem = pl.BlockSpec(memory_space=pltpu.VMEM)
        dma = pltpu.SemaphoreType.DMA
        out = jax.ShapeDtypeStruct((1, tile, rank), F32)
        return pl.pallas_call(
            functools.partial(kernel, n_row, n_col),
            out_shape=(out, out),
            in_specs=[vmem, pl.BlockSpec(memory_space=pltpu.SMEM), vmem, vmem, pl.BlockSpec(memory_space=pl.ANY), vmem],
            out_specs=(vmem, vmem),
            scratch_shapes=[
                pltpu.VMEM((tile, tile), F32),
                pltpu.VMEM((tile // rank, rank, rank), F32),
                pltpu.VMEM((tile, tile), BF16),
                pltpu.VMEM((tile, tile), BF16),
                pltpu.VMEM((tile, columns * rank), BF16),
                pltpu.VMEM((n_row, tile, columns * rank), BF16),
                pltpu.VMEM((slots * rank, columns * rank), F32),
                pltpu.VMEM((tile, rank), F32),
                pltpu.VMEM((tile, rank), F32),
                pltpu.VMEM((n_row - 1, chunk, rank), F32),
                pltpu.VMEM((tile, rank), F32),
                pltpu.VMEM((n_row, columns * rank, rank), F32),
                pltpu.VMEM((rank, rank), F32),
                dma(()),
                dma((n_col - 1,)), dma((n_col - 1,)),
                dma((n_col - 1,)), dma((n_col - 1,)),
                dma((n_row - 1,)), dma((n_row - 1,)),
                dma((n_row - 1, n_col - 1)), dma((n_row - 1, n_col - 1)),
                dma((n_row - 1,)), dma((n_row - 1,)),
                dma((n_row - 1,)), dma((n_row - 1,)),
                dma((n_row - 1,)), dma((n_row - 1,)),
            ],
            compiler_params=pltpu.CompilerParams(
                collective_id=0, has_side_effects=True, vmem_limit_bytes=56 * 1024 * 1024
            ),
            cost_estimate=pl.CostEstimate(flops=4 * 10**9, bytes_accessed=8 * 10**6, transcendentals=0),
        )(slot_factors, slot_pairs, pivot_factors, a_factors, diag_factor, sketch)

    in_specs = (
        P("row", "col", None, None, None),
        P("row", "col", None),
        P("row", "col", None),
        P("col", None, None),
        P(),
        P(),
    )
    out_specs = (P("col", None, None), P("col", None, None))
    return jax.shard_map(shards, mesh=mesh, in_specs=in_specs, out_specs=out_specs, check_vma=False)
```

time: 247 us -> 82.9 us (0.34); the launches traced: 243 us -> 81.7 us
  other arithmetic: 110 us -> 0 us
  Pallas kernels: 0 us -> 77.3 us
  waiting for transfers between devices: 55.5 us -> 0 us
  matrix products: 31.9 us -> 0 us
  local copies, waits for them, and re-layouts: 31.4 us -> 3.74 us
  between operations: 14.1 us -> 0.64 us
    another operation x9 -> x0, other arithmetic: 108 us -> none  [the longest x3 84.1 us: shards(): lax.linalg.triangular_solve(diag_factor, stacked, left_side=True, lower=T...]
    pallas_call x0 -> x1, Pallas kernels: none -> 77.3 us  [shards(): pl.pallas_call(functools.partial(kernel, n_row, n_col), out_shape=(out, o...]
    psum x2 -> x0, waiting for transfers between devices: 35.1 us -> none  [the longest x1 35.1 us: shards(): sketch_rows = y_a - lax.psum(y_part, 'row')]
    another operation x27 -> x0, local copies, waits for them, and re-layouts: 27.8 us -> none
    all_gather x1 -> x0, waiting for transfers between devices: 19.7 us -> none  [shards(): lax.all_gather(pivot_factors, 'col', axis=1, tiled=True).astype(jnp.float32)]
    dot_general x16 -> x0, matrix products: 18.2 us -> none  [the longest x1 2.73 us: shards(): jnp.einsum('st,sbd->tbd', tile_selector, lifted, precision=precise_mode)]
    another operation x16 -> x0, matrix products: 13.7 us -> none  [the longest x15 13.1 us: shards(): lax.linalg.triangular_solve(diag_factor, stacked, left_side=True, lower=T...]
    unnamed x17 -> x2, local copies, waits for them, and re-layouts: 1.12 us -> 3.74 us
  transfers between devices with their start and end apart: 3 -> 0, of which waited for: 2 -> 0; matrix products, arithmetic and copies ran while one was open for 48% -> 0% of each run, Pallas kernels for 0% -> 0%
where the time goes in v1:
time: 82.9 us; the launch traced here: 81.7 us
  Pallas kernels  77.3 us (93%)
  local copies, waits for them, and re-layouts  3.74 us (5%)
    pallas_call x1, Pallas kernels, shards(): pl.pallas_call(functools.partial(kernel, n_row, n_col), out_shape=(out, o...  77.3 us
    unnamed x2, local copies, waits for them, and re-layouts  3.74 us

profile of v1, /device:TPU:28, one launch (start us, length us, event | category | flops | bytes accessed | tf_op | source)
XLA Modules:
  0.0 81.7 jit_solution(2346803348470732732)
XLA Ops:
  0.6 77.3 %shard_map.77 = (f32[1,1024,128]{2,1,0:T(8,128)}, f32[1,1024,128]{2,1,0:T(8,128)}) custom-call(bf16[1,1,2,1024,256]{4,3,2,1,0:T(8,128)(2,1)} %slot_ref.1, s32[1,1,2]{2,1,0:T(1,128)} %pairs_ref.1, bf16[2,128,256]{2,1,0:T(8,128)(2,1)} %pivot_ref.1, bf16[1,1024,256]{2,1,0:T(8,128)(2,1)} %a_ref.1, f32[1024,1024]{1,0:T(8,128)} %diag_ref.1, f32[1024,128]{1,0:T(8,128)} %sketch_ref.1), custom_call_target="tpu_custom_call" | custom-call | flops 4000000000 | bytes 8000000 | tf_op jit(solution)/shard_map/pallas_call | solution.py:300
  77.9 1.9 %copy.10 = f32[1,1024,128]{2,1,0:T(8,128)} copy(f32[1,1024,128]{2,1,0:T(8,128)} %get-tuple-element.4) | data formatting | bytes 1048576
  79.8 1.9 %copy.11 = f32[1,1024,128]{2,1,0:T(8,128)} copy(f32[1,1024,128]{2,1,0:T(8,128)} %get-tuple-element.5) | data formatting | bytes 1048576

commit v2 on v1

--- a/solution.py
+++ b/solution.py
@@ -42,11 +42,11 @@
 def kernel(
     n_row, n_col,
     slot_ref, pairs_ref, pivot_ref, a_ref, diag_ref, sketch_ref,
-    basis_ref, coeff_ref,
+    sketched_ref, solved_ref, hinv_ref,
     diag_v, inv_small, inv_high, inv_low, pv_all, pu_all, coupling,
-    y_own, y_part, y_in, y_full, x_all, hinv,
-    diag_sem, pv_send, pv_recv, pu_send, pu_recv, pz_send, pz_recv,
-    pf_send, pf_recv, rs_send, rs_recv, ag_send, ag_recv, x_send, x_recv,
+    y_own, y_part, y_in, y_full, x_all,
+    diag_sem, pv_send, pv_recv, pu_send, pu_recv, sv_send, sv_recv, su_send, su_recv, pz_send, pz_recv,
+    pf_send, pf_recv, sf_send, sf_recv, rs_send, rs_recv, ag_send, ag_recv, x_send, x_recv,
 ):
     tile, rank = sketch_ref.shape
     columns, rows = pivot_ref.shape[0], pivot_ref.shape[1]
@@ -54,6 +54,9 @@
     chunk = tile // n_row
     r = lax.axis_index("row")
     c = lax.axis_index("col")
+    n_chip = n_col // 2
+    core, chip = lax.rem(c, 2), lax.div(c, 2)
+    sibling = c + 1 - 2 * core
 
     diag_copy = pltpu.make_async_copy(diag_ref, diag_v, diag_sem)
     diag_copy.start()
@@ -71,21 +74,31 @@
 
     barrier = pltpu.get_barrier_semaphore()
 
-    def greet_col(d, _):
-        pl.semaphore_signal(barrier, inc=1, device_id={"col": lax.rem(c + d, n_col)}, device_id_type=MESH)
+    def chip_mate(e):
+        return lax.rem(chip + e, n_chip) * 2 + core
+
+    def chip_source(e):
+        return lax.rem(chip + n_chip - e, n_chip) * 2 + core
+
+    def sibling_source(e):
+        return lax.rem(chip + n_chip - e, n_chip) * 2 + 1 - core
+
+    def greet_chip(e, _):
+        pl.semaphore_signal(barrier, inc=1, device_id={"col": chip_mate(e)}, device_id_type=MESH)
         return 0
 
     def greet_row(d, _):
         pl.semaphore_signal(barrier, inc=1, device_id={"row": lax.rem(r + d, n_row)}, device_id_type=MESH)
         return 0
 
-    lax.fori_loop(1, n_col, greet_col, 0)
+    lax.fori_loop(1, n_chip, greet_chip, 0)
     lax.fori_loop(1, n_row, greet_row, 0)
-    pl.semaphore_wait(barrier, n_col - 1 + n_row - 1)
-
-    def to_col(ref, send, recv, d):
+    pl.semaphore_signal(barrier, inc=1, device_id={"col": sibling}, device_id_type=MESH)
+    pl.semaphore_wait(barrier, n_chip - 1 + n_row - 1 + 1)
+
+    def to_col(ref, send, recv, target):
         return pltpu.make_async_remote_copy(
-            ref, ref, send, recv, device_id={"col": lax.rem(c + d, n_col)}, device_id_type=MESH
+            ref, ref, send, recv, device_id={"col": target}, device_id_type=MESH
         )
 
     def to_row(source, target, send, recv, d):
@@ -93,21 +106,29 @@
             source, target, send, recv, device_id={"row": lax.rem(r + d, n_row)}, device_id_type=MESH
         )
 
-    def pv_copy(d, index):
-        return to_col(pv_all.at[piece(index)], pv_send.at[d - 1], pv_recv.at[d - 1], d)
-
-    def pu_copy(d, index):
-        return to_col(pu_all.at[r, piece(index)], pu_send.at[d - 1], pu_recv.at[d - 1], d)
+    def pv_copy(e, index):
+        return to_col(pv_all.at[piece(index)], pv_send.at[e - 1], pv_recv.at[e - 1], chip_mate(e))
+
+    def pu_copy(e, index):
+        return to_col(pu_all.at[r, piece(index)], pu_send.at[e - 1], pu_recv.at[e - 1], chip_mate(e))
+
+    def sv_copy(e, index):
+        return to_col(pv_all.at[piece(index)], sv_send.at[e], sv_recv.at[e], sibling)
+
+    def su_copy(e, index):
+        return to_col(pu_all.at[r, piece(index)], su_send.at[e], su_recv.at[e], sibling)
 
     def pz_copy(d, index):
         ref = pu_all.at[index, piece(c)]
         return to_row(ref, ref, pz_send.at[d - 1], pz_recv.at[d - 1], d)
 
-    def pf_copy(e, d, index):
-        from_row = lax.rem(r + n_row - e, n_row)
-        return to_col(
-            pu_all.at[from_row, piece(index)], pf_send.at[e - 1, d - 1], pf_recv.at[e - 1, d - 1], d
-        )
+    def pf_copy(d, e, index):
+        ref = pu_all.at[row_source(d), piece(index)]
+        return to_col(ref, pf_send.at[d - 1, e - 1], pf_recv.at[d - 1, e - 1], chip_mate(e))
+
+    def sf_copy(d, e, index):
+        ref = pu_all.at[row_source(d), piece(index)]
+        return to_col(ref, sf_send.at[d - 1, e], sf_recv.at[d - 1, e], sibling)
 
     def rs_copy(d):
         return to_row(
@@ -122,9 +143,6 @@
         ref = x_all.at[index]
         return to_row(ref, ref, x_send.at[d - 1], x_recv.at[d - 1], d)
 
-    def col_source(d):
-        return lax.rem(c + n_col - d, n_col)
-
     def row_source(d):
         return lax.rem(r + n_row - d, n_row)
 
@@ -135,11 +153,13 @@
 
         lax.fori_loop(1, n, body, 0)
 
-    def push_pivots(d):
-        pv_copy(d, c).start()
-        pu_copy(d, c).start()
-
-    each(n_col, push_pivots)
+    def push_pivots(e):
+        pv_copy(e, c).start()
+        pu_copy(e, c).start()
+
+    each(n_chip, push_pivots)
+    sv_copy(0, c).start()
+    su_copy(0, c).start()
     each(n_row, lambda d: pz_copy(d, r).start())
 
     sketch_split = split(sketch_ref[...])
@@ -147,6 +167,12 @@
     a_right = a_ref[0, :, rank:]
     a_sketch = dot(a_right, sketch_split[0], TN) + dot(a_right, sketch_split[1], TN)
     y_own[...] = dot_exact_left(a_left, a_sketch)
+
+    def pass_pivots(e):
+        pv_copy(e, chip_source(e)).wait_recv()
+        sv_copy(e, chip_source(e)).start()
+        pu_copy(e, chip_source(e)).wait_recv()
+        su_copy(e, chip_source(e)).start()
 
     diag_copy.wait()
     blocks = tile // rank
@@ -177,10 +203,17 @@
             inv_small[b] = now - dot_split(split(dot_split(now_split, cross)), now_split)
         return 0
 
-    lax.fori_loop(1, rank.bit_length() - 1, double, 0)
-
-    each(n_col, lambda d: pv_copy(d, col_source(d)).wait_recv())
-    each(n_col, lambda d: pu_copy(d, col_source(d)).wait_recv())
+    levels = rank.bit_length() - 1
+    lax.fori_loop(1, levels // 2 + 1, double, 0)
+    each(n_chip, pass_pivots)
+    lax.fori_loop(levels // 2 + 1, levels, double, 0)
+
+    def take_pivots(e):
+        sv_copy(e, sibling_source(e)).wait_recv()
+        su_copy(e, sibling_source(e)).wait_recv()
+
+    take_pivots(0)
+    each(n_chip, take_pivots)
     pivot_right = pv_all[...]
     for s in range(slots):
         code = pairs_ref[0, 0, s]
@@ -191,15 +224,28 @@
     pivot_left = pu_all[r]
     weights = dot(pivot_left, sketch_split[0], TN) + dot(pivot_left, sketch_split[1], TN)
     mixed = dot_wide(coupling[...], weights)
-    total = dot_exact_left(slot_ref[0, 0, 0, :, :rank], mixed[:rank])
-    for s in range(1, slots):
-        total += dot_exact_left(slot_ref[0, 0, s, :, :rank], mixed[s * rank:(s + 1) * rank])
-    y_part[...] = total
-    each(n_row, lambda d: rs_copy(d).start())
-
-    def forward(e):
-        pz_copy(e, row_source(e)).wait_recv()
-        each(n_col, lambda d: pf_copy(e, d, c).start())
+    mixed_split = split(mixed)
+
+    def update_rows(index):
+        span = part(index)
+        total = jnp.zeros((chunk, rank), F32)
+        for s in range(slots):
+            left = slot_ref[0, 0, s, span, :rank]
+            for half in mixed_split:
+                total += dot(left, half[s * rank:(s + 1) * rank])
+        y_part[span] = total
+
+    def push_update(d):
+        update_rows(lax.rem(r + d, n_row))
+        rs_copy(d).start()
+
+    each(n_row, push_update)
+    update_rows(r)
+
+    def forward(d):
+        pz_copy(d, row_source(d)).wait_recv()
+        each(n_chip, lambda e: pf_copy(d, e, c).start())
+        sf_copy(d, 0, c).start()
 
     each(n_row, forward)
 
@@ -228,62 +274,106 @@
         mine = mine - y_in[d - 1]
     y_full[part(r)] = mine
     each(n_row, lambda d: ag_copy(d, r).start())
+
+    def pass_forward(d, e):
+        pf_copy(d, e, chip_source(e)).wait_recv()
+        sf_copy(d, e, chip_source(e)).start()
+
+    each(n_row, lambda d: each(n_chip, lambda e: pass_forward(d, e)))
     each(n_row, lambda d: ag_copy(d, row_source(d)).wait_recv())
 
     sketched = y_full[...]
+    sketched_ref[...] = sketched
     sketched_split = split(sketched)
-    gram = lax.dot_general(sketched, sketched, TN, precision=lax.Precision.HIGHEST, preferred_element_type=F32)
-    state = jnp.concatenate([gram, jnp.where(on_diag, 1.0, 0.0)], axis=1)
-    group = 8
-    sub_group = lax.broadcasted_iota(jnp.int32, (group, 1), 0)
-    lane_group = lax.broadcasted_iota(jnp.int32, (group, 2 * rank), 1)
-    sub_wide = lax.broadcasted_iota(jnp.int32, (group, 2 * rank), 0)
-    for start in range(0, rank, group):
-        block = state[start:start + group]
-        for t in range(group - 1):
-            k = start + t
-            factor = block[:, k:k + 1] / block[t:t + 1, k:k + 1]
-            block = block - jnp.where(sub_group > t, factor, 0.0) * block[t:t + 1]
-        pivots = jnp.sum(jnp.where(lane_group == sub_wide + start, block, 0.0), axis=1, keepdims=True)
-        block = block * lax.rsqrt(pivots)
-        hinv[start:start + group] = block[:, rank:]
-        if start + group < rank:
-            left = jnp.where(lane_group[:, :rank] >= start + group, block[:, :rank], 0.0)
-            state = state - dot_wide(left, block, TN)
-
-    basis_split = split(dot_split(sketched_split, split(hinv[...]), NT))
-    basis = basis_split[0].astype(F32) + basis_split[1].astype(F32)
 
     def across(left):
-        return dot(left, basis_split[0], TN) + dot(left, basis_split[1], TN)
+        return dot(left, sketched_split[0], TN) + dot(left, sketched_split[1], TN)
 
     inner = jnp.concatenate([across(slot_ref[0, 0, s, :, :rank]) for s in range(slots)], axis=0)
     x_all[r] = dot_wide(coupling[...], inner, TN)
     each(n_row, lambda d: x_copy(d, r).start())
-
-    root = float(tile) ** 0.5
-    basis_ref[0] = basis * root
-    projected = dot_exact_left(a_right, across(a_left))
-    each(n_row, lambda e: each(n_col, lambda d: pf_copy(e, d, col_source(d)).wait_recv()))
+    solved_ref[...] = dot_exact_left(a_right, across(a_left))
+
+    gram = lax.dot_general(sketched, sketched, TN, precision=lax.Precision.HIGHEST, preferred_element_type=F32)
+    state_gram, state_eye = gram, jnp.where(on_diag, 1.0, 0.0)
+    group = 16
+    sub_group = lax.broadcasted_iota(jnp.int32, (group, rank), 0)
+    lane_group = lax.broadcasted_iota(jnp.int32, (group, rank), 1)
+    for start in range(0, rank, group):
+        block = state_gram[start:start + group]
+        eye = state_eye[start:start + group]
+        cols = [
+            jnp.broadcast_to(block[:, start + u:start + u + 1], (group, rank)) for u in range(group)
+        ]
+        pivots = jnp.zeros((group, rank), F32)
+        for t in range(group):
+            pivot = cols[t][t:t + 1]
+            pivots = jnp.where(sub_group == t, pivot, pivots)
+            if t + 1 < group:
+                factor = jnp.where(sub_group > t, cols[t] * (1.0 / pivot), 0.0)
+                for u in range(t + 1, group):
+                    cols[u] = cols[u] - factor * cols[u][t:t + 1]
+                block = block - factor * block[t:t + 1]
+                eye = eye - factor * eye[t:t + 1]
+        scale = lax.rsqrt(pivots)
+        block = block * scale
+        eye = eye * scale
+        hinv_ref[start:start + group] = eye
+        if start + group < rank:
+            left_high, left_low = split(jnp.where(lane_group >= start + group, block, 0.0))
+            block_high, block_low = split(block)
+            eye_high, eye_low = split(eye)
+            left = jnp.concatenate([left_high, left_high, left_low, left_low], axis=0)
+            state_gram = state_gram - dot(
+                left, jnp.concatenate([block_high, block_low, block_high, block_low], axis=0), TN
+            )
+            state_eye = state_eye - dot(
+                left, jnp.concatenate([eye_high, eye_low, eye_high, eye_low], axis=0), TN
+            )
+
+    projected = solved_ref[...]
+
+    def take_forward(d):
+        sf_copy(d, 0, sibling_source(0)).wait_recv()
+        each(n_chip, lambda e: sf_copy(d, e, sibling_source(e)).wait_recv())
+
+    each(n_row, take_forward)
     each(n_row, lambda d: x_copy(d, row_source(d)).wait_recv())
     for row in range(n_row):
         projected = projected - dot_exact_left(pu_all[row], x_all[row])
-    projected_split = split(projected)
-    coeff_ref[0] = dot_split((inv_high[...], inv_low[...]), projected_split) * (1.0 / root)
-
-    def finish_col(d):
-        pv_copy(d, c).wait_send()
-        pu_copy(d, c).wait_send()
+    solved_ref[...] = dot_split((inv_high[...], inv_low[...]), split(projected))
+
+    def finish_chip(e):
+        pv_copy(e, c).wait_send()
+        pu_copy(e, c).wait_send()
+
+    def finish_sibling(e):
+        sv_copy(e, chip_source(e)).wait_send()
+        su_copy(e, chip_source(e)).wait_send()
 
     def finish_row(d):
         pz_copy(d, r).wait_send()
         rs_copy(d).wait_send()
         ag_copy(d, r).wait_send()
         x_copy(d, r).wait_send()
-
-    each(n_col, finish_col)
+        sf_copy(d, 0, c).wait_send()
+
+    def finish_forward(d, e):
+        pf_copy(d, e, c).wait_send()
+        sf_copy(d, e, chip_source(e)).wait_send()
+
+    each(n_chip, finish_chip)
+    finish_sibling(0)
+    each(n_chip, finish_sibling)
     each(n_row, finish_row)
-    each(n_row, lambda e: each(n_col, lambda d: pf_copy(e, d, c).wait_send()))
+    each(n_row, lambda d: each(n_chip, lambda e: finish_forward(d, e)))
+
+
+def scale_kernel(sketched_ref, solved_ref, hinv_ref, basis_ref, coeff_ref):
+    root = float(sketched_ref.shape[0]) ** 0.5
+    factor = split(hinv_ref[...])
+    basis_ref[0] = dot_split(split(sketched_ref[...]), factor, NT) * root
+    coeff_ref[0] = dot_split(split(solved_ref[...]), factor, NT) * (1.0 / root)
 
 
 def solution(mesh):
@@ -297,11 +387,13 @@
         vmem = pl.BlockSpec(memory_space=pltpu.VMEM)
         dma = pltpu.SemaphoreType.DMA
         out = jax.ShapeDtypeStruct((1, tile, rank), F32)
-        return pl.pallas_call(
+        n_chip = n_col // 2
+        wide = jax.ShapeDtypeStruct((tile, rank), F32)
+        sketched, solved, hinv = pl.pallas_call(
             functools.partial(kernel, n_row, n_col),
-            out_shape=(out, out),
+            out_shape=(wide, wide, jax.ShapeDtypeStruct((rank, rank), F32)),
             in_specs=[vmem, pl.BlockSpec(memory_space=pltpu.SMEM), vmem, vmem, pl.BlockSpec(memory_space=pl.ANY), vmem],
-            out_specs=(vmem, vmem),
+            out_specs=(vmem, vmem, vmem),
             scratch_shapes=[
                 pltpu.VMEM((tile, tile), F32),
                 pltpu.VMEM((tile // rank, rank, rank), F32),
@@ -315,12 +407,14 @@
                 pltpu.VMEM((n_row - 1, chunk, rank), F32),
                 pltpu.VMEM((tile, rank), F32),
                 pltpu.VMEM((n_row, columns * rank, rank), F32),
-                pltpu.VMEM((rank, rank), F32),
                 dma(()),
-                dma((n_col - 1,)), dma((n_col - 1,)),
-                dma((n_col - 1,)), dma((n_col - 1,)),
+                dma((n_chip - 1,)), dma((n_chip - 1,)),
+                dma((n_chip - 1,)), dma((n_chip - 1,)),
+                dma((n_chip,)), dma((n_chip,)),
+                dma((n_chip,)), dma((n_chip,)),
                 dma((n_row - 1,)), dma((n_row - 1,)),
-                dma((n_row - 1, n_col - 1)), dma((n_row - 1, n_col - 1)),
+                dma((n_row - 1, n_chip - 1)), dma((n_row - 1, n_chip - 1)),
+                dma((n_row - 1, n_chip)), dma((n_row - 1, n_chip)),
                 dma((n_row - 1,)), dma((n_row - 1,)),
                 dma((n_row - 1,)), dma((n_row - 1,)),
                 dma((n_row - 1,)), dma((n_row - 1,)),
@@ -330,6 +424,13 @@
             ),
             cost_estimate=pl.CostEstimate(flops=4 * 10**9, bytes_accessed=8 * 10**6, transcendentals=0),
         )(slot_factors, slot_pairs, pivot_factors, a_factors, diag_factor, sketch)
+        return pl.pallas_call(
+            scale_kernel,
+            out_shape=(out, out),
+            in_specs=[vmem, vmem, vmem],
+            out_specs=(vmem, vmem),
+            compiler_params=pltpu.CompilerParams(vmem_limit_bytes=24 * 1024 * 1024),
+        )(sketched, solved, hinv)
 
     in_specs = (
         P("row", "col", None, None, None),

time: 82.9 us -> 64.8 us (0.78)
  the two profiles are of different devices: /device:TPU:28 before, /device:TPU:0 now
where the time goes in v2:
time: 64.8 us; the launch traced here: 64.5 us
  Pallas kernels  60.9 us (94%)
  local copies, waits for them, and re-layouts  2.91 us (4%)
  between operations  0.65 us (1%)
    pallas_call x1, Pallas kernels, shards(): pl.pallas_call(functools.partial(kernel, n_row, n_col), out_shape=(wide,...  59.4 us
    unnamed x6, local copies, waits for them, and re-layouts  2.91 us
    pallas_call x1, Pallas kernels, shards(): pl.pallas_call(scale_kernel, out_shape=(out, out), in_specs=[vmem, vmem,...  1.55 us

profile of v2, /device:TPU:0, one launch (start us, length us, event | category | flops | bytes accessed | tf_op | source)
XLA Modules:
  0.0 64.5 jit_solution(10200798252675397275)
XLA Ops:
  0.6 59.4 %shard_map.77 = (f32[1024,128]{1,0:T(8,128)}, f32[1024,128]{1,0:T(8,128)}, f32[128,128]{1,0:T(8,128)}) custom-call(bf16[1,1,2,1024,256]{4,3,2,1,0:T(8,128)(2,1)} %slot_ref.1, s32[1,1,2]{2,1,0:T(1,128)} %pairs_ref.1, bf16[2,128,256]{2,1,0:T(8,128)(2,1)} %pivot_ref.1, bf16[1,1024,256]{2,1,0:T(8,128)(2,1)} %a_ref.1, f32[1024,1024]{1,0:T(8,128)} %diag_ref.1, ...), custom_call_target="tpu_custom_call" | custom-call | flops 4000000000 | bytes 8000000 | tf_op jit(solution)/shard_map/pallas_call | solution.py:392
  60.0 0.0 copy-start
  60.0 1.0 %copy-done = f32[1024,128]{1,0:T(8,128)S(1)} copy-done((f32[1024,128]{1,0:T(8,128)S(1)}, f32[1024,128]{1,0:T(8,128)}, u32[]{:S(2)}) %copy-start) | copy-done | bytes 524312
  61.0 0.0 copy-start.1
  61.0 1.0 %copy-done.1 = f32[1024,128]{1,0:T(8,128)S(1)} copy-done((f32[1024,128]{1,0:T(8,128)S(1)}, f32[1024,128]{1,0:T(8,128)}, u32[]{:S(2)}) %copy-start.1) | copy-done | bytes 524312
  62.1 0.0 copy-start.2
  62.1 0.8 %copy-done.2 = f32[128,128]{1,0:T(8,128)S(1)} copy-done((f32[128,128]{1,0:T(8,128)S(1)}, f32[128,128]{1,0:T(8,128)}, u32[]{:S(2)}) %copy-start.2) | copy-done | bytes 65560
  62.9 1.6 %shard_map.78 = (f32[1,1024,128]{2,1,0:T(8,128)}, f32[1,1024,128]{2,1,0:T(8,128)}) custom-call(f32[1024,128]{1,0:T(8,128)S(1)} %copy-done, f32[1024,128]{1,0:T(8,128)S(1)} %copy-done.1, f32[128,128]{1,0:T(8,128)S(1)} %copy-done.2), custom_call_target="tpu_custom_call" | custom-call | tf_op jit(solution)/shard_map/pallas_call | solution.py:427
Async XLA Ops:
  60.0 1.0 %copy-start = (f32[1024,128]{1,0:T(8,128)S(1)}, f32[1024,128]{1,0:T(8,128)}, u32[]{:S(2)}) copy-start(f32[1024,128]{1,0:T(8,128)} %get-tuple-element.5.sketched_ref) | copy-start | bytes 1572868
  61.0 1.0 %copy-start.1 = (f32[1024,128]{1,0:T(8,128)S(1)}, f32[1024,128]{1,0:T(8,128)}, u32[]{:S(2)}) copy-start(f32[1024,128]{1,0:T(8,128)} %get-tuple-element.6.solved_ref) | copy-start | bytes 1572868
  62.1 0.8 %copy-start.2 = (f32[128,128]{1,0:T(8,128)S(1)}, f32[128,128]{1,0:T(8,128)}, u32[]{:S(2)}) copy-start(f32[128,128]{1,0:T(8,128)} %get-tuple-element.7.hinv_ref) | copy-start | bytes 196612

commit v3 on v2

--- a/solution.py
+++ b/solution.py
@@ -41,11 +41,11 @@
 
 def kernel(
     n_row, n_col,
-    slot_ref, pairs_ref, pivot_ref, a_ref, diag_ref, sketch_ref,
+    slot_hbm, pairs_ref, pivot_ref, a_hbm, diag_ref, sketch_hbm,
     sketched_ref, solved_ref, hinv_ref,
-    diag_v, inv_small, inv_high, inv_low, pv_all, pu_all, coupling,
-    y_own, y_part, y_in, y_full, x_all,
-    diag_sem, pv_send, pv_recv, pu_send, pu_recv, sv_send, sv_recv, su_send, su_recv, pz_send, pz_recv,
+    slot_ref, a_ref, sketch_ref, diag_v, inv_small, inv_high, inv_low, pv_all, pu_all, coupling,
+    y_own, y_part, y_in, y_full, x_all, gram_v, inner_v,
+    slot_sem, a_sem, sketch_sem, diag_sem, pv_send, pv_recv, pu_send, pu_recv, sv_send, sv_recv, su_send, su_recv, pz_send, pz_recv,
     pf_send, pf_recv, sf_send, sf_recv, rs_send, rs_recv, ag_send, ag_recv, x_send, x_recv,
 ):
     tile, rank = sketch_ref.shape
@@ -58,8 +58,14 @@
     core, chip = lax.rem(c, 2), lax.div(c, 2)
     sibling = c + 1 - 2 * core
 
+    a_copy = pltpu.make_async_copy(a_hbm, a_ref, a_sem)
+    sketch_copy = pltpu.make_async_copy(sketch_hbm, sketch_ref, sketch_sem)
+    slot_copy = pltpu.make_async_copy(slot_hbm, slot_ref, slot_sem)
     diag_copy = pltpu.make_async_copy(diag_ref, diag_v, diag_sem)
+    a_copy.start()
+    sketch_copy.start()
     diag_copy.start()
+    slot_copy.start()
 
     def piece(index):
         return pl.ds(pl.multiple_of(index * rows, rows), rows)
@@ -162,6 +168,8 @@
     su_copy(0, c).start()
     each(n_row, lambda d: pz_copy(d, r).start())
 
+    sketch_copy.wait()
+    a_copy.wait()
     sketch_split = split(sketch_ref[...])
     a_left = a_ref[0, :, :rank]
     a_right = a_ref[0, :, rank:]
@@ -204,9 +212,10 @@
         return 0
 
     levels = rank.bit_length() - 1
-    lax.fori_loop(1, levels // 2 + 1, double, 0)
+    early = 3
+    lax.fori_loop(1, early, double, 0)
     each(n_chip, pass_pivots)
-    lax.fori_loop(levels // 2 + 1, levels, double, 0)
+    slot_copy.wait()
 
     def take_pivots(e):
         sv_copy(e, sibling_source(e)).wait_recv()
@@ -248,6 +257,33 @@
         sf_copy(d, 0, c).start()
 
     each(n_row, forward)
+
+    lax.fori_loop(early, levels, double, 0)
+
+    each(n_row, lambda d: rs_copy(d).wait_recv())
+    mine = y_own[part(r)] - y_part[part(r)]
+    for d in range(1, n_row):
+        mine = mine - y_in[d - 1]
+    y_full[part(r)] = mine
+    each(n_row, lambda d: ag_copy(d, r).start())
+
+    def pass_forward(d, e):
+        pf_copy(d, e, chip_source(e)).wait_recv()
+        sf_copy(d, e, chip_source(e)).start()
+
+    each(n_row, lambda d: each(n_chip, lambda e: pass_forward(d, e)))
+
+    def products(index):
+        span = part(index)
+        piece_y = y_full[span]
+        lefts = [slot_ref[0, 0, s, span, :rank] for s in range(slots)] + [a_ref[0, span, :rank]]
+        inner = dot_exact_left(jnp.concatenate(lefts, axis=1), piece_y, TN)
+        gram = lax.dot_general(
+            piece_y, piece_y, TN, precision=lax.Precision.HIGHEST, preferred_element_type=F32
+        )
+        return inner, gram
+
+    inner_v[...], gram_v[...] = products(r)
 
     inv_high[...] = jnp.zeros_like(inv_high)
     inv_low[...] = jnp.zeros_like(inv_low)
@@ -268,34 +304,19 @@
             inv_low[second, first] = low
         size *= 2
 
-    each(n_row, lambda d: rs_copy(d).wait_recv())
-    mine = y_own[part(r)] - y_part[part(r)]
-    for d in range(1, n_row):
-        mine = mine - y_in[d - 1]
-    y_full[part(r)] = mine
-    each(n_row, lambda d: ag_copy(d, r).start())
-
-    def pass_forward(d, e):
-        pf_copy(d, e, chip_source(e)).wait_recv()
-        sf_copy(d, e, chip_source(e)).start()
-
-    each(n_row, lambda d: each(n_chip, lambda e: pass_forward(d, e)))
-    each(n_row, lambda d: ag_copy(d, row_source(d)).wait_recv())
-
-    sketched = y_full[...]
-    sketched_ref[...] = sketched
-    sketched_split = split(sketched)
-
-    def across(left):
-        return dot(left, sketched_split[0], TN) + dot(left, sketched_split[1], TN)
-
-    inner = jnp.concatenate([across(slot_ref[0, 0, s, :, :rank]) for s in range(slots)], axis=0)
-    x_all[r] = dot_wide(coupling[...], inner, TN)
+    def take_chunk(d):
+        ag_copy(d, row_source(d)).wait_recv()
+        inner, gram = products(row_source(d))
+        inner_v[...] += inner
+        gram_v[...] += gram
+
+    each(n_row, take_chunk)
+    x_all[r] = dot_wide(coupling[...], inner_v[:slots * rank], TN)
     each(n_row, lambda d: x_copy(d, r).start())
-    solved_ref[...] = dot_exact_left(a_right, across(a_left))
-
-    gram = lax.dot_general(sketched, sketched, TN, precision=lax.Precision.HIGHEST, preferred_element_type=F32)
-    state_gram, state_eye = gram, jnp.where(on_diag, 1.0, 0.0)
+    sketched_ref[...] = y_full[...]
+    solved_ref[...] = dot_exact_left(a_right, inner_v[slots * rank:]) - dot_exact_left(pu_all[r], x_all[r])
+
+    state_gram, state_eye = gram_v[...], jnp.where(on_diag, 1.0, 0.0)
     group = 16
     sub_group = lax.broadcasted_iota(jnp.int32, (group, rank), 0)
     lane_group = lax.broadcasted_iota(jnp.int32, (group, rank), 1)
@@ -331,17 +352,18 @@
                 left, jnp.concatenate([eye_high, eye_low, eye_high, eye_low], axis=0), TN
             )
 
-    projected = solved_ref[...]
-
-    def take_forward(d):
+    def take_product(d):
         sf_copy(d, 0, sibling_source(0)).wait_recv()
         each(n_chip, lambda e: sf_copy(d, e, sibling_source(e)).wait_recv())
-
-    each(n_row, take_forward)
-    each(n_row, lambda d: x_copy(d, row_source(d)).wait_recv())
-    for row in range(n_row):
-        projected = projected - dot_exact_left(pu_all[row], x_all[row])
-    solved_ref[...] = dot_split((inv_high[...], inv_low[...]), split(projected))
+        x_copy(d, row_source(d)).wait_recv()
+        solved_ref[...] -= dot_exact_left(pu_all[row_source(d)], x_all[row_source(d)])
+
+    each(n_row, take_product)
+    high, low = split(solved_ref[...])
+    band = 2 * rank
+    for start in range(0, tile, band):
+        span, upto = slice(start, start + band), slice(0, start + band)
+        solved_ref[span] = dot_split((inv_high[span, upto], inv_low[span, upto]), (high[upto], low[upto]))
 
     def finish_chip(e):
         pv_copy(e, c).wait_send()
@@ -385,6 +407,7 @@
         slots = slot_factors.shape[2]
         chunk = tile // n_row
         vmem = pl.BlockSpec(memory_space=pltpu.VMEM)
+        hbm = pl.BlockSpec(memory_space=pl.ANY)
         dma = pltpu.SemaphoreType.DMA
         out = jax.ShapeDtypeStruct((1, tile, rank), F32)
         n_chip = n_col // 2
@@ -392,9 +415,12 @@
         sketched, solved, hinv = pl.pallas_call(
             functools.partial(kernel, n_row, n_col),
             out_shape=(wide, wide, jax.ShapeDtypeStruct((rank, rank), F32)),
-            in_specs=[vmem, pl.BlockSpec(memory_space=pltpu.SMEM), vmem, vmem, pl.BlockSpec(memory_space=pl.ANY), vmem],
+            in_specs=[hbm, pl.BlockSpec(memory_space=pltpu.SMEM), vmem, hbm, hbm, hbm],
             out_specs=(vmem, vmem, vmem),
             scratch_shapes=[
+                pltpu.VMEM(slot_factors.shape, BF16),
+                pltpu.VMEM(a_factors.shape, BF16),
+                pltpu.VMEM((tile, rank), F32),
                 pltpu.VMEM((tile, tile), F32),
                 pltpu.VMEM((tile // rank, rank, rank), F32),
                 pltpu.VMEM((tile, tile), BF16),
@@ -407,7 +433,9 @@
                 pltpu.VMEM((n_row - 1, chunk, rank), F32),
                 pltpu.VMEM((tile, rank), F32),
                 pltpu.VMEM((n_row, columns * rank, rank), F32),
-                dma(()),
+                pltpu.VMEM((rank, rank), F32),
+                pltpu.VMEM(((slots + 1) * rank, rank), F32),
+                dma(()), dma(()), dma(()), dma(()),
                 dma((n_chip - 1,)), dma((n_chip - 1,)),
                 dma((n_chip - 1,)), dma((n_chip - 1,)),
                 dma((n_chip,)), dma((n_chip,)),
@@ -420,7 +448,7 @@
                 dma((n_row - 1,)), dma((n_row - 1,)),
             ],
             compiler_params=pltpu.CompilerParams(
-                collective_id=0, has_side_effects=True, vmem_limit_bytes=56 * 1024 * 1024
+                collective_id=0, has_side_effects=True, vmem_limit_bytes=60 * 1024 * 1024
             ),
             cost_estimate=pl.CostEstimate(flops=4 * 10**9, bytes_accessed=8 * 10**6, transcendentals=0),
         )(slot_factors, slot_pairs, pivot_factors, a_factors, diag_factor, sketch)
@@ -429,7 +457,7 @@
             out_shape=(out, out),
             in_specs=[vmem, vmem, vmem],
             out_specs=(vmem, vmem),
-            compiler_params=pltpu.CompilerParams(vmem_limit_bytes=24 * 1024 * 1024),
+            compiler_params=pltpu.CompilerParams(vmem_limit_bytes=60 * 1024 * 1024),
         )(sketched, solved, hinv)
 
     in_specs = (

time: 64.8 us -> 59 us (0.910)
  the two profiles are of different devices: /device:TPU:0 before, /device:TPU:28 now
where the time goes in v3:
time: 59 us; the launch traced here: 58.3 us
  Pallas kernels  57.6 us (98%)
  between operations  0.64 us (1%)
    pallas_call x1, Pallas kernels, shards(): pl.pallas_call(functools.partial(kernel, n_row, n_col), out_shape=(wide,...  54.9 us
    pallas_call x1, Pallas kernels, shards(): pl.pallas_call(scale_kernel, out_shape=(out, out), in_specs=[vmem, vmem,...  2.76 us

profile of v3, /device:TPU:28, one launch (start us, length us, event | category | flops | bytes accessed | tf_op | source)
XLA Modules:
  0.0 58.3 jit_solution(5098126072280299142)
XLA Ops:
  0.6 54.9 %shard_map.77 = (f32[1024,128]{1,0:T(8,128)}, f32[1024,128]{1,0:T(8,128)}, f32[128,128]{1,0:T(8,128)}) custom-call(bf16[1,1,2,1024,256]{4,3,2,1,0:T(8,128)(2,1)} %slot_hbm.1, s32[1,1,2]{2,1,0:T(1,128)} %pairs_ref.1, bf16[2,128,256]{2,1,0:T(8,128)(2,1)} %pivot_ref.1, bf16[1,1024,256]{2,1,0:T(8,128)(2,1)} %a_hbm.1, f32[1024,1024]{1,0:T(8,128)} %diag_ref.1, ...), custom_call_target="tpu_custom_call" | custom-call | flops 4000000000 | bytes 8000000 | tf_op jit(solution)/shard_map/pallas_call | solution.py:415
  55.5 2.8 %shard_map.78 = (f32[1,1024,128]{2,1,0:T(8,128)}, f32[1,1024,128]{2,1,0:T(8,128)}) custom-call(f32[1024,128]{1,0:T(8,128)} %get-tuple-element.5.sketched_ref, f32[1024,128]{1,0:T(8,128)} %get-tuple-element.6.solved_ref, f32[128,128]{1,0:T(8,128)} %get-tuple-element.7.hinv_ref), custom_call_target="tpu_custom_call" | custom-call | tf_op jit(solution)/shard_map/pallas_call | solution.py:455

commit v4 on v3

--- a/solution.py
+++ b/solution.py
@@ -7,6 +7,7 @@
 from jax.experimental.pallas import tpu as pltpu
 from jax.sharding import PartitionSpec as P
 
+HALVES = 2
 MESH = pl.DeviceIdType.MESH
 F32 = jnp.float32
 BF16 = jnp.bfloat16
@@ -52,6 +53,7 @@
     columns, rows = pivot_ref.shape[0], pivot_ref.shape[1]
     slots = slot_ref.shape[2]
     chunk = tile // n_row
+    half = chunk // HALVES
     r = lax.axis_index("row")
     c = lax.axis_index("col")
     n_chip = n_col // 2
@@ -70,8 +72,8 @@
     def piece(index):
         return pl.ds(pl.multiple_of(index * rows, rows), rows)
 
-    def part(index):
-        return pl.ds(pl.multiple_of(index * chunk, chunk), chunk)
+    def part(index, h):
+        return pl.ds(pl.multiple_of(index * chunk + h * half, half), half)
 
     for j in range(columns):
         lanes = slice(j * rank, (j + 1) * rank)
@@ -136,14 +138,15 @@
         ref = pu_all.at[row_source(d), piece(index)]
         return to_col(ref, sf_send.at[d - 1, e], sf_recv.at[d - 1, e], sibling)
 
-    def rs_copy(d):
+    def rs_copy(d, h):
         return to_row(
-            y_part.at[part(lax.rem(r + d, n_row))], y_in.at[d - 1], rs_send.at[d - 1], rs_recv.at[d - 1], d
+            y_part.at[part(lax.rem(r + d, n_row), h)], y_in.at[d - 1, h],
+            rs_send.at[d - 1, h], rs_recv.at[d - 1, h], d,
         )
 
-    def ag_copy(d, index):
-        ref = y_full.at[part(index)]
-        return to_row(ref, ref, ag_send.at[d - 1], ag_recv.at[d - 1], d)
+    def ag_copy(d, index, h):
+        ref = y_full.at[part(index, h)]
+        return to_row(ref, ref, ag_send.at[d - 1, h], ag_recv.at[d - 1, h], d)
 
     def x_copy(d, index):
         ref = x_all.at[index]
@@ -235,21 +238,23 @@
     mixed = dot_wide(coupling[...], weights)
     mixed_split = split(mixed)
 
-    def update_rows(index):
-        span = part(index)
-        total = jnp.zeros((chunk, rank), F32)
+    def update_rows(index, h):
+        span = part(index, h)
+        total = jnp.zeros((half, rank), F32)
         for s in range(slots):
             left = slot_ref[0, 0, s, span, :rank]
-            for half in mixed_split:
-                total += dot(left, half[s * rank:(s + 1) * rank])
+            for term in mixed_split:
+                total += dot(left, term[s * rank:(s + 1) * rank])
         y_part[span] = total
 
-    def push_update(d):
-        update_rows(lax.rem(r + d, n_row))
-        rs_copy(d).start()
-
-    each(n_row, push_update)
-    update_rows(r)
+    def push_update(d, h):
+        update_rows(lax.rem(r + d, n_row), h)
+        rs_copy(d, h).start()
+
+    for h in range(HALVES):
+        each(n_row, lambda d: push_update(d, h))
+    for h in range(HALVES):
+        update_rows(r, h)
 
     def forward(d):
         pz_copy(d, row_source(d)).wait_recv()
@@ -260,12 +265,13 @@
 
     lax.fori_loop(early, levels, double, 0)
 
-    each(n_row, lambda d: rs_copy(d).wait_recv())
-    mine = y_own[part(r)] - y_part[part(r)]
-    for d in range(1, n_row):
-        mine = mine - y_in[d - 1]
-    y_full[part(r)] = mine
-    each(n_row, lambda d: ag_copy(d, r).start())
+    for h in range(HALVES):
+        each(n_row, lambda d: rs_copy(d, h).wait_recv())
+        mine = y_own[part(r, h)] - y_part[part(r, h)]
+        for d in range(1, n_row):
+            mine = mine - y_in[d - 1, h]
+        y_full[part(r, h)] = mine
+        each(n_row, lambda d: ag_copy(d, r, h).start())
 
     def pass_forward(d, e):
         pf_copy(d, e, chip_source(e)).wait_recv()
@@ -273,8 +279,8 @@
 
     each(n_row, lambda d: each(n_chip, lambda e: pass_forward(d, e)))
 
-    def products(index):
-        span = part(index)
+    def products(index, h):
+        span = part(index, h)
         piece_y = y_full[span]
         lefts = [slot_ref[0, 0, s, span, :rank] for s in range(slots)] + [a_ref[0, span, :rank]]
         inner = dot_exact_left(jnp.concatenate(lefts, axis=1), piece_y, TN)
@@ -283,7 +289,16 @@
         )
         return inner, gram
 
-    inner_v[...], gram_v[...] = products(r)
+    inner_v[...] = jnp.zeros_like(inner_v)
+    gram_v[...] = jnp.zeros_like(gram_v)
+
+    def add_products(index, h):
+        inner, gram = products(index, h)
+        inner_v[...] += inner
+        gram_v[...] += gram
+
+    for h in range(HALVES):
+        add_products(r, h)
 
     inv_high[...] = jnp.zeros_like(inv_high)
     inv_low[...] = jnp.zeros_like(inv_low)
@@ -304,13 +319,12 @@
             inv_low[second, first] = low
         size *= 2
 
-    def take_chunk(d):
-        ag_copy(d, row_source(d)).wait_recv()
-        inner, gram = products(row_source(d))
-        inner_v[...] += inner
-        gram_v[...] += gram
-
-    each(n_row, take_chunk)
+    def take_chunk(d, h):
+        ag_copy(d, row_source(d), h).wait_recv()
+        add_products(row_source(d), h)
+
+    for h in range(HALVES):
+        each(n_row, lambda d: take_chunk(d, h))
     x_all[r] = dot_wide(coupling[...], inner_v[:slots * rank], TN)
     each(n_row, lambda d: x_copy(d, r).start())
     sketched_ref[...] = y_full[...]
@@ -375,8 +389,9 @@
 
     def finish_row(d):
         pz_copy(d, r).wait_send()
-        rs_copy(d).wait_send()
-        ag_copy(d, r).wait_send()
+        for h in range(HALVES):
+            rs_copy(d, h).wait_send()
+            ag_copy(d, r, h).wait_send()
         x_copy(d, r).wait_send()
         sf_copy(d, 0, c).wait_send()
 
@@ -391,8 +406,7 @@
     each(n_row, lambda d: each(n_chip, lambda e: finish_forward(d, e)))
 
 
-def scale_kernel(sketched_ref, solved_ref, hinv_ref, basis_ref, coeff_ref):
-    root = float(sketched_ref.shape[0]) ** 0.5
+def scale_kernel(root, sketched_ref, solved_ref, hinv_ref, basis_ref, coeff_ref):
     factor = split(hinv_ref[...])
     basis_ref[0] = dot_split(split(sketched_ref[...]), factor, NT) * root
     coeff_ref[0] = dot_split(split(solved_ref[...]), factor, NT) * (1.0 / root)
@@ -430,7 +444,7 @@
                 pltpu.VMEM((slots * rank, columns * rank), F32),
                 pltpu.VMEM((tile, rank), F32),
                 pltpu.VMEM((tile, rank), F32),
-                pltpu.VMEM((n_row - 1, chunk, rank), F32),
+                pltpu.VMEM((n_row - 1, HALVES, chunk // HALVES, rank), F32),
                 pltpu.VMEM((tile, rank), F32),
                 pltpu.VMEM((n_row, columns * rank, rank), F32),
                 pltpu.VMEM((rank, rank), F32),
@@ -443,8 +457,8 @@
                 dma((n_row - 1,)), dma((n_row - 1,)),
                 dma((n_row - 1, n_chip - 1)), dma((n_row - 1, n_chip - 1)),
                 dma((n_row - 1, n_chip)), dma((n_row - 1, n_chip)),
-                dma((n_row - 1,)), dma((n_row - 1,)),
-                dma((n_row - 1,)), dma((n_row - 1,)),
+                dma((n_row - 1, HALVES)), dma((n_row - 1, HALVES)),
+                dma((n_row - 1, HALVES)), dma((n_row - 1, HALVES)),
                 dma((n_row - 1,)), dma((n_row - 1,)),
             ],
             compiler_params=pltpu.CompilerParams(
@@ -453,10 +467,18 @@
             cost_estimate=pl.CostEstimate(flops=4 * 10**9, bytes_accessed=8 * 10**6, transcendentals=0),
         )(slot_factors, slot_pairs, pivot_factors, a_factors, diag_factor, sketch)
         return pl.pallas_call(
-            scale_kernel,
+            functools.partial(scale_kernel, float(tile) ** 0.5),
             out_shape=(out, out),
-            in_specs=[vmem, vmem, vmem],
-            out_specs=(vmem, vmem),
+            grid=(4,),
+            in_specs=[
+                pl.BlockSpec((tile // 4, rank), lambda i: (i, 0)),
+                pl.BlockSpec((tile // 4, rank), lambda i: (i, 0)),
+                pl.BlockSpec((rank, rank), lambda i: (0, 0)),
+            ],
+            out_specs=(
+                pl.BlockSpec((1, tile // 4, rank), lambda i: (0, i, 0)),
+                pl.BlockSpec((1, tile // 4, rank), lambda i: (0, i, 0)),
+            ),
             compiler_params=pltpu.CompilerParams(vmem_limit_bytes=60 * 1024 * 1024),
         )(sketched, solved, hinv)
 

time: 59 us -> 59.8 us (1.014)
  Pallas kernels: 57.6 us -> 58.9 us
    pallas_call x1, Pallas kernels: 2.76 us -> 3.92 us  [shards(): pl.pallas_call(functools.partial(scale_kernel, float(tile) ** 0.5), out_s...]
where the time goes in v4:
time: 59.8 us; the launch traced here: 59.6 us
  Pallas kernels  58.9 us (98%)
  between operations  0.64 us (1%)
    pallas_call x1, Pallas kernels, shards(): pl.pallas_call(functools.partial(kernel, n_row, n_col), out_shape=(wide,...  55 us
    pallas_call x1, Pallas kernels, shards(): pl.pallas_call(functools.partial(scale_kernel, float(tile) ** 0.5), out_s...  3.92 us

profile of v4, /device:TPU:28, one launch (start us, length us, event | category | flops | bytes accessed | tf_op | source)
XLA Modules:
  0.0 59.6 jit_solution(17242450018177862287)
XLA Ops:
  0.6 55.0 %shard_map.77 = (f32[1024,128]{1,0:T(8,128)}, f32[1024,128]{1,0:T(8,128)}, f32[128,128]{1,0:T(8,128)}) custom-call(bf16[1,1,2,1024,256]{4,3,2,1,0:T(8,128)(2,1)} %slot_hbm.1, s32[1,1,2]{2,1,0:T(1,128)} %pairs_ref.1, bf16[2,128,256]{2,1,0:T(8,128)(2,1)} %pivot_ref.1, bf16[1,1024,256]{2,1,0:T(8,128)(2,1)} %a_hbm.1, f32[1024,1024]{1,0:T(8,128)} %diag_ref.1, ...), custom_call_target="tpu_custom_call" | custom-call | flops 4000000000 | bytes 8000000 | tf_op jit(solution)/shard_map/pallas_call | solution.py:429
  55.6 3.9 %shard_map.78 = (f32[1,1024,128]{2,1,0:T(8,128)}, f32[1,1024,128]{2,1,0:T(8,128)}) custom-call(f32[1024,128]{1,0:T(8,128)} %get-tuple-element.5.sketched_ref, f32[1024,128]{1,0:T(8,128)} %get-tuple-element.6.solved_ref, f32[128,128]{1,0:T(8,128)} %get-tuple-element.7.hinv_ref), custom_call_target="tpu_custom_call" | custom-call | tf_op jit(solution)/shard_map/pallas_call | solution.py:469

commit v5 on v4

--- a/solution.py
+++ b/solution.py
@@ -25,15 +25,24 @@
     return lax.dot_general(a, b, dims, preferred_element_type=F32)
 
 
+def fold(x):
+    width = x.shape[1] // 2
+    return x[:, :width] + x[:, width:]
+
+
 def dot_exact_left(a, b, dims=NN):
-    high, low = split(b)
-    return dot(a, high, dims) + dot(a, low, dims)
+    return fold(dot(a, jnp.concatenate(split(b), axis=1), dims))
 
 
 def dot_split(a, b, dims=NN):
     a_high, a_low = a
     b_high, b_low = b
-    return dot(a_high, b_high, dims) + (dot(a_high, b_low, dims) + dot(a_low, b_high, dims))
+    if dims == NT or b_high.shape[1] > 128:
+        return dot(a_high, b_high, dims) + (dot(a_high, b_low, dims) + dot(a_low, b_high, dims))
+    both = jnp.concatenate([b_high, b_low], axis=1)
+    if dims == NN and b_high.shape[0] <= 128:
+        return fold(dot(jnp.concatenate([a_high, a_low], axis=1), jnp.concatenate([both, both], axis=0)))
+    return fold(dot(a_high, both, dims)) + dot(a_low, b_high, dims)
 
 
 def dot_wide(a, b, dims=NN):
@@ -281,13 +290,11 @@
 
     def products(index, h):
         span = part(index, h)
-        piece_y = y_full[span]
+        halves = split(y_full[span])
         lefts = [slot_ref[0, 0, s, span, :rank] for s in range(slots)] + [a_ref[0, span, :rank]]
-        inner = dot_exact_left(jnp.concatenate(lefts, axis=1), piece_y, TN)
-        gram = lax.dot_general(
-            piece_y, piece_y, TN, precision=lax.Precision.HIGHEST, preferred_element_type=F32
-        )
-        return inner, gram
+        whole = fold(dot(jnp.concatenate([*lefts, *halves], axis=1), jnp.concatenate(halves, axis=1), TN))
+        edge = (slots + 1) * rank
+        return whole[:edge], whole[edge:edge + rank] + whole[edge + rank:]
 
     inner_v[...] = jnp.zeros_like(inner_v)
     gram_v[...] = jnp.zeros_like(gram_v)
@@ -469,16 +476,8 @@
         return pl.pallas_call(
             functools.partial(scale_kernel, float(tile) ** 0.5),
             out_shape=(out, out),
-            grid=(4,),
-            in_specs=[
-                pl.BlockSpec((tile // 4, rank), lambda i: (i, 0)),
-                pl.BlockSpec((tile // 4, rank), lambda i: (i, 0)),
-                pl.BlockSpec((rank, rank), lambda i: (0, 0)),
-            ],
-            out_specs=(
-                pl.BlockSpec((1, tile // 4, rank), lambda i: (0, i, 0)),
-                pl.BlockSpec((1, tile // 4, rank), lambda i: (0, i, 0)),
-            ),
+            in_specs=[vmem, vmem, vmem],
+            out_specs=(vmem, vmem),
             compiler_params=pltpu.CompilerParams(vmem_limit_bytes=60 * 1024 * 1024),
         )(sketched, solved, hinv)
 

time: 59.8 us -> 57.8 us (0.967)
  Pallas kernels: 58.9 us -> 57 us
    pallas_call x1, Pallas kernels: 3.92 us -> 2.76 us  [shards(): pl.pallas_call(functools.partial(scale_kernel, float(tile) ** 0.5), out_s...]
    pallas_call x1, Pallas kernels: 55 us -> 54.2 us  [shards(): pl.pallas_call(functools.partial(kernel, n_row, n_col), out_shape=(wide,...]
where the time goes in v5:
time: 57.8 us; the launch traced here: 57.6 us
  Pallas kernels  57 us (99%)
  between operations  0.64 us (1%)
    pallas_call x1, Pallas kernels, shards(): pl.pallas_call(functools.partial(kernel, n_row, n_col), out_shape=(wide,...  54.2 us
    pallas_call x1, Pallas kernels, shards(): pl.pallas_call(functools.partial(scale_kernel, float(tile) ** 0.5), out_s...  2.76 us

profile of v5, /device:TPU:28, one launch (start us, length us, event | category | flops | bytes accessed | tf_op | source)
XLA Modules:
  0.0 57.6 jit_solution(17304953568168872870)
XLA Ops:
  0.6 54.2 %shard_map.77 = (f32[1024,128]{1,0:T(8,128)}, f32[1024,128]{1,0:T(8,128)}, f32[128,128]{1,0:T(8,128)}) custom-call(bf16[1,1,2,1024,256]{4,3,2,1,0:T(8,128)(2,1)} %slot_hbm.1, s32[1,1,2]{2,1,0:T(1,128)} %pairs_ref.1, bf16[2,128,256]{2,1,0:T(8,128)(2,1)} %pivot_ref.1, bf16[1,1024,256]{2,1,0:T(8,128)(2,1)} %a_hbm.1, f32[1024,1024]{1,0:T(8,128)} %diag_ref.1, ...), custom_call_target="tpu_custom_call" | custom-call | flops 4000000000 | bytes 8000000 | tf_op jit(solution)/shard_map/pallas_call | solution.py:436
  54.9 2.8 %shard_map.78 = (f32[1,1024,128]{2,1,0:T(8,128)}, f32[1,1024,128]{2,1,0:T(8,128)}) custom-call(f32[1024,128]{1,0:T(8,128)} %get-tuple-element.5.sketched_ref, f32[1024,128]{1,0:T(8,128)} %get-tuple-element.6.solved_ref, f32[128,128]{1,0:T(8,128)} %get-tuple-element.7.hinv_ref), custom_call_target="tpu_custom_call" | custom-call | tf_op jit(solution)/shard_map/pallas_call | solution.py:476

commit v6 on v5

--- a/solution.py
+++ b/solution.py
@@ -339,24 +339,37 @@
 
     state_gram, state_eye = gram_v[...], jnp.where(on_diag, 1.0, 0.0)
     group = 16
-    sub_group = lax.broadcasted_iota(jnp.int32, (group, rank), 0)
+    sub_half = lax.broadcasted_iota(jnp.int32, (8, rank), 0)
+    tops = range(0, group, 8)
     lane_group = lax.broadcasted_iota(jnp.int32, (group, rank), 1)
     for start in range(0, rank, group):
-        block = state_gram[start:start + group]
-        eye = state_eye[start:start + group]
+        block = [state_gram[start + p:start + p + 8] for p in tops]
+        eye = [state_eye[start + p:start + p + 8] for p in tops]
         cols = [
-            jnp.broadcast_to(block[:, start + u:start + u + 1], (group, rank)) for u in range(group)
+            [jnp.broadcast_to(piece[:, start + u:start + u + 1], (8, rank)) for piece in block]
+            for u in range(group)
         ]
-        pivots = jnp.zeros((group, rank), F32)
+        pivots = [jnp.ones((8, rank), F32) for _ in tops]
         for t in range(group):
-            pivot = cols[t][t:t + 1]
-            pivots = jnp.where(sub_group == t, pivot, pivots)
-            if t + 1 < group:
-                factor = jnp.where(sub_group > t, cols[t] * (1.0 / pivot), 0.0)
+            own, row = t // 8, slice(t % 8, t % 8 + 1)
+            pivot = cols[t][own][row]
+            pivots[own] = jnp.where(sub_half == t % 8, pivot, pivots[own])
+            inverse = 1.0 / pivot
+            heads = [cols[u][own][row] for u in range(t + 1, group)]
+            head_block, head_eye = block[own][row], eye[own][row]
+            for p in range(own, len(block)):
+                if p == own and t % 8 == 7:
+                    continue
+                factor = cols[t][p] * inverse
+                if p == own:
+                    factor = jnp.where(sub_half > t % 8, factor, 0.0)
                 for u in range(t + 1, group):
-                    cols[u] = cols[u] - factor * cols[u][t:t + 1]
-                block = block - factor * block[t:t + 1]
-                eye = eye - factor * eye[t:t + 1]
+                    cols[u][p] = cols[u][p] - factor * heads[u - t - 1]
+                block[p] = block[p] - factor * head_block
+                eye[p] = eye[p] - factor * head_eye
+        block = jnp.concatenate(block, axis=0)
+        eye = jnp.concatenate(eye, axis=0)
+        pivots = jnp.concatenate(pivots, axis=0)
         scale = lax.rsqrt(pivots)
         block = block * scale
         eye = eye * scale

time: 57.8 us -> 57.8 us (level)
  no operation moved by 1% of the time
where the time goes in v6:
time: 57.8 us; the launch traced here: 57.6 us
  Pallas kernels  57 us (99%)
  between operations  0.64 us (1%)
    pallas_call x1, Pallas kernels, shards(): pl.pallas_call(functools.partial(kernel, n_row, n_col), out_shape=(wide,...  54.2 us
    pallas_call x1, Pallas kernels, shards(): pl.pallas_call(functools.partial(scale_kernel, float(tile) ** 0.5), out_s...  2.76 us

profile of v6, /device:TPU:28, one launch (start us, length us, event | category | flops | bytes accessed | tf_op | source)
XLA Modules:
  0.0 57.6 jit_solution(1981034693820584150)
XLA Ops:
  0.6 54.2 %shard_map.77 = (f32[1024,128]{1,0:T(8,128)}, f32[1024,128]{1,0:T(8,128)}, f32[128,128]{1,0:T(8,128)}) custom-call(bf16[1,1,2,1024,256]{4,3,2,1,0:T(8,128)(2,1)} %slot_hbm.1, s32[1,1,2]{2,1,0:T(1,128)} %pairs_ref.1, bf16[2,128,256]{2,1,0:T(8,128)(2,1)} %pivot_ref.1, bf16[1,1024,256]{2,1,0:T(8,128)(2,1)} %a_hbm.1, f32[1024,1024]{1,0:T(8,128)} %diag_ref.1, ...), custom_call_target="tpu_custom_call" | custom-call | flops 4000000000 | bytes 8000000 | tf_op jit(solution)/shard_map/pallas_call | solution.py:449
  54.9 2.8 %shard_map.78 = (f32[1,1024,128]{2,1,0:T(8,128)}, f32[1,1024,128]{2,1,0:T(8,128)}) custom-call(f32[1024,128]{1,0:T(8,128)} %get-tuple-element.5.sketched_ref, f32[1024,128]{1,0:T(8,128)} %get-tuple-element.6.solved_ref, f32[128,128]{1,0:T(8,128)} %get-tuple-element.7.hinv_ref), custom_call_target="tpu_custom_call" | custom-call | tf_op jit(solution)/shard_map/pallas_call | solution.py:489

commit v7 on v5

--- a/solution.py
+++ b/solution.py
@@ -225,8 +225,8 @@
 
     levels = rank.bit_length() - 1
     early = 3
+    each(n_chip, pass_pivots)
     lax.fori_loop(1, early, double, 0)
-    each(n_chip, pass_pivots)
     slot_copy.wait()
 
     def take_pivots(e):

time: 57.8 us -> 58.7 us (1.016)
  the two profiles are of different devices: /device:TPU:28 before, /device:TPU:0 now
where the time goes in v7:
time: 58.7 us; the launch traced here: 58.5 us
  Pallas kernels  57.9 us (99%)
  between operations  0.64 us (1%)
    pallas_call x1, Pallas kernels, shards(): pl.pallas_call(functools.partial(kernel, n_row, n_col), out_shape=(wide,...  55.1 us
    pallas_call x1, Pallas kernels, shards(): pl.pallas_call(functools.partial(scale_kernel, float(tile) ** 0.5), out_s...  2.76 us

profile of v7, /device:TPU:0, one launch (start us, length us, event | category | flops | bytes accessed | tf_op | source)
XLA Modules:
  0.0 58.5 jit_solution(5253349442604244388)
XLA Ops:
  0.6 55.1 %shard_map.77 = (f32[1024,128]{1,0:T(8,128)}, f32[1024,128]{1,0:T(8,128)}, f32[128,128]{1,0:T(8,128)}) custom-call(bf16[1,1,2,1024,256]{4,3,2,1,0:T(8,128)(2,1)} %slot_hbm.1, s32[1,1,2]{2,1,0:T(1,128)} %pairs_ref.1, bf16[2,128,256]{2,1,0:T(8,128)(2,1)} %pivot_ref.1, bf16[1,1024,256]{2,1,0:T(8,128)(2,1)} %a_hbm.1, f32[1024,1024]{1,0:T(8,128)} %diag_ref.1, ...), custom_call_target="tpu_custom_call" | custom-call | flops 4000000000 | bytes 8000000 | tf_op jit(solution)/shard_map/pallas_call | solution.py:436
  55.8 2.8 %shard_map.78 = (f32[1,1024,128]{2,1,0:T(8,128)}, f32[1,1024,128]{2,1,0:T(8,128)}) custom-call(f32[1024,128]{1,0:T(8,128)} %get-tuple-element.5.sketched_ref, f32[1024,128]{1,0:T(8,128)} %get-tuple-element.6.solved_ref, f32[128,128]{1,0:T(8,128)} %get-tuple-element.7.hinv_ref), custom_call_target="tpu_custom_call" | custom-call | tf_op jit(solution)/shard_map/pallas_call | solution.py:476
